TPU v7x, 128 devices: a whole 4x4x4 slice. The times are simulated.
128 devices in a mesh: tm: 8 (over x_lo, z), height: 16 (over y, x_hi, core).
Axes of the slice: x: 4 (x_hi: 2, x_lo: 2; x = x_hi * 2 + x_lo), y: 4, z: 4, core: 2. Of those that a mesh axis runs over, the one named last changes fastest.
Arguments:
- queries: bfloat16 [32, 32, 16, 2560], P('tm', 'height'), may hold values from -64 to 64
- keys: bfloat16 [32, 32, 16, 2560], P('tm', 'height'), may hold values from -64 to 64
- values: bfloat16 [32, 32, 16, 2560], P('tm', 'height'), may hold values from -6 to 6
- tile_mask: int32 [8, 16, 2, 18], P('tm', 'height'), may hold values 0 or 1
- sink_frame: int32 [1], replicated, may hold values from 0 to 31
Outputs:
- attended: bfloat16 [32, 32, 16, 2560], P('tm', 'height')
All inputs are finite; a program needn't handle non-finite values. No bound on the sum of `tile_mask` on one device may be relied on, other than what follows from the above.
Results may differ from a plain program's by a relative error of at most 0.0041.
Values may be sent and summed in bfloat16 or wider, within the bound.
A program may use at most 128 MiB of HBM per device.

v0:
```python
import math

import jax
import jax.numpy as jnp
from jax import lax
from jax.sharding import PartitionSpec as P

H = 20
HD = 128
TF = 4
TC = 8


masked_score = -1e30


def from_behind(value, axis, steps):
    count = lax.axis_size(axis)
    first, last = (max(0, -steps), min(count, count - steps))
    return lax.ppermute(value, axis, [(source, source + steps) for source in range(first, last)])


def with_halo(cells, sides, width):
    for axis, dim in sides:
        count = lax.axis_size(axis)
        ends = count - 1
        head = lax.slice_in_dim(cells, 0, width, axis=dim)
        tail = lax.slice_in_dim(cells, cells.shape[dim] - width, cells.shape[dim], axis=dim)
        cells = jnp.concatenate(
            [
                lax.ppermute(tail, axis, [(i, (i + 1) % count) for i in range(ends)]),
                cells,
                lax.ppermute(head, axis, [((i + 1) % count, i) for i in range(ends)]),
            ],
            axis=dim,
        )
    return cells


def from_root(x, axis, root):
    mine = lax.axis_index(axis) == root
    return lax.psum(jnp.where(mine, x, jnp.zeros_like(x)), axis)


def near_allowed(tile_flags, time_base, band_index, band_total):
    q_tiles = tile_flags.shape[0]
    w_tiles = tile_flags.shape[1]
    q_time = jnp.arange(q_tiles)[:, None, None, None, None]
    q_width = jnp.arange(w_tiles)[None, :, None, None, None]
    slot = jnp.arange(2)[None, None, :, None, None]
    k_band = jnp.arange(3)[None, None, None, :, None] - 1
    width_slot = jnp.arange(3)[None, None, None, None, :]
    code_all = slot * 9 + (k_band + 1) * 3 + width_slot
    matches = code_all[..., None] == jnp.arange(tile_flags.shape[2])
    picked = jnp.sum(jnp.where(matches, tile_flags[:, :, None, None, None, :], 0), axis=-1) > 0
    itself = (slot == 1) & (k_band == 0) & (width_slot == 1)
    time_valid = time_base + q_time + slot - 1 >= 0
    band_now = band_index + k_band
    band_valid = (band_now >= 0) & (band_now < band_total)
    col_now = q_width + width_slot - 1
    col_valid = (col_now >= 0) & (col_now < w_tiles)
    return (picked | itself) & time_valid & band_valid & col_valid


def token_allowed(tiles_ok, row_count):
    q_tiles, w_tiles = (tiles_ok.shape[0], tiles_ok.shape[1])
    tile_tokens = TF * row_count * TC
    grid = tiles_ok[:, :, None, :, None, :, None, :, None]
    full = jnp.broadcast_to(grid, (q_tiles, w_tiles, tile_tokens, 2, TF, 3, row_count, 3, TC))
    return full.reshape(q_tiles, w_tiles, tile_tokens, 2 * TF * 3 * row_count * 3 * TC)


def shards(queries, keys, values, tile_mask, sink_frame):
    frames, row_count, col_count, features = queries.shape
    head_count = H
    scaling = 1.0 / math.sqrt(HD)
    local_tiles = frames // TF
    width_tiles = col_count // TC
    tile_tokens = TF * row_count * TC
    token_count = frames * row_count * col_count
    key_vals = jnp.stack((keys, values))
    prior_keys = from_behind(key_vals, "tm", 1)
    joined = jnp.concatenate((prior_keys, key_vals), axis=1)
    window = with_halo(joined, (("height", 2),), row_count)
    q_tiled = queries.reshape(local_tiles, TF, row_count, width_tiles, TC, head_count, HD)
    q_tiled = jnp.transpose(q_tiled, (0, 3, 1, 2, 4, 5, 6)).reshape(
        local_tiles, width_tiles, tile_tokens, head_count, HD
    )
    q_flat = q_tiled.reshape(token_count, head_count, HD)
    tiles_ok = near_allowed(
        tile_mask[:, 0],
        lax.axis_index("tm") * local_tiles,
        lax.axis_index("height"),
        lax.axis_size("height"),
    )
    allowed = token_allowed(tiles_ok, row_count)
    group_size = math.gcd(head_count, 4)
    group_count = head_count // group_size

    def head_step(step_no, running):
        run_max, run_sum, summed = running
        offset = step_no * group_size
        q_part = lax.dynamic_slice_in_dim(q_tiled, offset, group_size, 3)
        win_part = lax.dynamic_slice_in_dim(window, offset * HD, group_size * HD, 4)
        padded = jnp.pad(win_part, ((0, 0), (0, 0), (0, 0), (TC, TC), (0, 0)))
        tiled = padded.reshape(
            2, local_tiles + 1, TF, 3 * row_count, col_count + 2 * TC, group_size * HD
        )
        paired = jnp.stack((tiled[:, :-1], tiled[:, 1:]), axis=2)
        shifted = jnp.stack(
            [
                paired[:, :, :, :, :, shift_no * TC : shift_no * TC + col_count]
                for shift_no in range(3)
            ],
            axis=5,
        )
        shifted = shifted.reshape(
            2, local_tiles, 2, TF, 3, row_count, 3, width_tiles, TC, group_size, HD
        )
        shifted = jnp.transpose(shifted, (0, 1, 7, 2, 3, 4, 5, 6, 8, 9, 10))
        shifted = shifted.reshape(2, local_tiles, width_tiles, -1, group_size, HD)
        scores = (
            jnp.einsum("tcqhd,tckhd->tchqk", q_part, shifted[0], preferred_element_type=jnp.float32)
            * scaling
        )
        scores = jnp.where(allowed[:, :, None], scores, masked_score)
        row_max = jnp.max(scores, axis=-1)
        weights = jnp.exp(scores - row_max[..., None]).astype(jnp.bfloat16)
        row_sum = jnp.sum(weights, axis=-1, dtype=jnp.float32)
        partial_out = jnp.einsum(
            "tchqk,tckhd->tcqhd", weights, shifted[1], preferred_element_type=jnp.float32
        )
        row_max = jnp.transpose(row_max, (2, 0, 1, 3)).reshape(group_size, token_count)
        row_sum = jnp.transpose(row_sum, (2, 0, 1, 3)).reshape(group_size, token_count)
        partial_out = partial_out.reshape(token_count, group_size, HD)
        run_max = lax.dynamic_update_slice_in_dim(run_max, row_max, offset, 0)
        run_sum = lax.dynamic_update_slice_in_dim(run_sum, row_sum, offset, 0)
        summed = lax.dynamic_update_slice_in_dim(summed, partial_out, offset, 1)
        return (run_max, run_sum, summed)

    window_init = (
        jnp.zeros((head_count, token_count), jnp.float32),
        jnp.zeros((head_count, token_count), jnp.float32),
        jnp.zeros((token_count, head_count, HD), jnp.float32),
    )
    win_max, win_sum, win_out = lax.fori_loop(0, group_count, head_step, window_init)
    sink_init = (
        jnp.full((head_count, token_count), masked_score, jnp.float32),
        jnp.zeros((head_count, token_count), jnp.float32),
        jnp.zeros((token_count, head_count, HD), jnp.float32),
    )
    owner_index = sink_frame[0] // frames
    local_frame = sink_frame[0] % frames
    sink_piece = lax.dynamic_slice_in_dim(key_vals, local_frame, 1, 1)[:, 0]
    whole_sink = lax.all_gather(sink_piece, "height", axis=1, tiled=True)
    whole_sink = from_root(whole_sink, "tm", owner_index)
    shard_rows = whole_sink
    band_total = shard_rows.shape[1] // row_count

    def band_step(step_no, state):
        run_max, run_sum, summed = state
        block_rows = lax.dynamic_slice_in_dim(shard_rows, step_no * row_count, row_count, 1)
        key_block = block_rows[0].reshape(row_count * col_count, head_count, HD)
        val_block = block_rows[1].reshape(row_count * col_count, head_count, HD)
        scores = (
            jnp.einsum("qhd,khd->hqk", q_flat, key_block, preferred_element_type=jnp.float32)
            * scaling
        )
        row_max = jnp.max(scores, axis=-1)
        weights = jnp.exp(scores - row_max[..., None]).astype(jnp.bfloat16)
        row_sum = jnp.sum(weights, axis=-1, dtype=jnp.float32)
        added = jnp.einsum("hqk,khd->qhd", weights, val_block, preferred_element_type=jnp.float32)
        new_max = jnp.maximum(run_max, row_max)
        keep_old = jnp.exp(run_max - new_max)
        factor = jnp.exp(row_max - new_max)
        run_sum = run_sum * keep_old + row_sum * factor
        summed = summed * keep_old.T[..., None] + added * factor.T[..., None]
        return (new_max, run_sum, summed)

    sink_max, sink_sum, sink_out = lax.fori_loop(0, band_total, band_step, sink_init)
    top_score = jnp.maximum(win_max, sink_max)
    win_factor = jnp.exp(win_max - top_score)
    sink_factor = jnp.exp(sink_max - top_score)
    denominator = win_factor * win_sum + sink_factor * sink_sum
    numerator = win_out * win_factor.T[..., None] + sink_out * sink_factor.T[..., None]
    result = (numerator / denominator.T[..., None]).astype(jnp.bfloat16)
    result = result.reshape(local_tiles, width_tiles, TF, row_count, TC, features)
    result = jnp.transpose(result, (0, 2, 3, 1, 4, 5))
    return result.reshape(frames, row_count, col_count, features)


def solution(mesh):
    return jax.shard_map(
        shards,
        mesh=mesh,
        in_specs=(
            P("tm", "height", None, None),
            P("tm", "height", None, None),
            P("tm", "height", None, None),
            P("tm", "height", None, None),
            P(),
        ),
        out_specs=P("tm", "height", None, None),
        check_vma=False,
    )
```

profile of v0, /device:TPU:1, one launch (start us, length us, event | category | flops | bytes accessed | tf_op | source)
XLA Modules:
  0.0 343.3 jit_solution(5612537318182779095)
XLA Ops:
  7.4 1.8 fusion.16
  9.4 4.5 %collective-permute-start = (bf16[2,4,2,16,2560]{4,3,2,0,1:T(8,128)(2,1)S(1)}, bf16[2,4,2,16,2560]{4,3,2,0,1:T(8,128)(2,1)S(1)}, u32[]{:S(2)}, u32[]{:S(2)}) collective-permute-start(bf16[2,4,2,16,2560]{4,3,2,0,1:T(8,128)(2,1)S(1)} %pad_maximum_fusion.2), channel_id=1, source_target_pairs={{0,16},{16,32},{32,48},{48,64},{64,80},{80,96},{96,112},{1,17},{17... | collective-permute-start | bytes 3932168 | tf_op jit(solution)/shard_map/ppermute | solution.py:20
  13.8 27.3 %collective-permute-done = bf16[2,4,2,16,2560]{4,3,2,0,1:T(8,128)(2,1)S(1)} collective-permute-done((bf16[2,4,2,16,2560]{4,3,2,0,1:T(8,128)(2,1)S(1)}, bf16[2,4,2,16,2560]{4,3,2,0,1:T(8,128)(2,1)S(1)}, u32[]{:S(2)}, u32[]{:S(2)}) %collective-permute-start) | collective-permute-done | bytes 1310752 | tf_op jit(solution)/shard_map/ppermute | solution.py:20
  41.2 1.8 maximum_maximum_fusion
  42.9 6.1 %collective-permute-start.1 = (bf16[2,8,2,16,2560]{4,3,2,0,1:T(8,128)(2,1)}, bf16[2,8,2,16,2560]{4,3,2,0,1:T(8,128)(2,1)}, u32[]{:S(2)}, u32[]{:S(2)}) collective-permute-start(bf16[2,8,2,16,2560]{4,3,2,0,1:T(8,128)(2,1)} %maximum_maximum_fusion), channel_id=1, source_target_pairs={{0,1},{1,2},{2,3},{3,4},{4,5},{5,6},{6,7},{7,8},{8,9},{9,10},{10,1... | collective-permute-start | bytes 7864328 | tf_op jit(solution)/shard_map/ppermute | solution.py:31
  49.0 1.9 collective-permute-start.2
  52.1 1.2 copy_bitcast_fusion.1
  54.2 36.8 %collective-permute-done.1 = bf16[2,8,2,16,2560]{4,3,2,0,1:T(8,128)(2,1)} collective-permute-done((bf16[2,8,2,16,2560]{4,3,2,0,1:T(8,128)(2,1)}, bf16[2,8,2,16,2560]{4,3,2,0,1:T(8,128)(2,1)}, u32[]{:S(2)}, u32[]{:S(2)}) %collective-permute-start.1) | collective-permute-done | bytes 2621472 | tf_op jit(solution)/shard_map/ppermute | solution.py:31
  91.0 30.7 %collective-permute-done.2 = bf16[2,8,2,16,2560]{4,3,2,0,1:T(8,128)(2,1)} collective-permute-done((bf16[2,8,2,16,2560]{4,3,2,0,1:T(8,128)(2,1)}, bf16[2,8,2,16,2560]{4,3,2,0,1:T(8,128)(2,1)}, u32[]{:S(2)}, u32[]{:S(2)}) %collective-permute-start.2) | collective-permute-done | bytes 2621472 | tf_op jit(solution)/shard_map/ppermute | solution.py:33
  121.7 6.3 %pad_maximum_fusion.1 = bf16[2,8,6,16,2560]{4,3,2,0,1:T(8,128)(2,1)} fusion(bf16[2,8,2,16,2560]{4,3,2,0,1:T(8,128)(2,1)} %collective-permute-done.2, bf16[1,4,2,16,2560]{4,3,2,0,1:T(8,128)(2,1)S(1)} %bitcast.139, bf16[1,4,2,16,2560]{4,3,2,0,1:T(8,128)(2,1)S(1)} %bitcast.135, bf16[2,4,2,16,2560]{4,3,2,0,1:T(8,128)(2,1)S(1)} %collective-permute-done, ...), kind=kLoop, calls=%fused_computation.42 | loop fusion | flops 15728640 | bytes 15728640 | tf_op jit(solution)/shard_map/concatenate | solution.py:29
  128.0 2.6 select_bitcast_fusion
  130.7 1.3 broadcast.330.clone.1
  132.0 75.1 %while.38 = (s32[]{:T(128)}, f32[20,128]{1,0:T(8,128)S(1)}, f32[20,128]{1,0:T(8,128)S(1)}, f32[128,20,128]{0,2,1:T(8,128)}, bf16[1,2,64,20,128]{4,2,3,1,0:T(8,12...) while((s32[]{:T(128)}, f32[20,128]{1,0:T(8,128)S(1)}, ...), condition=%wide.region_4.5_spmd.clone, body=%wide.region_1.4_spmd.clone.sunk | while | flops 321453056 | bytes 86737208 | solution.py:146
  132.0 1.5 constant_dynamic-slice_fusion.5
  135.9 2.5 fusion.44
  138.4 2.0 copy.127
  141.0 3.4 fusion.45
  147.3 1.5 constant_dynamic-slice_fusion.5
  151.2 2.5 fusion.44
  153.7 2.0 copy.127
  156.3 3.0 fusion.45
  162.2 1.6 constant_dynamic-slice_fusion.5
  166.2 2.5 fusion.44
  168.6 2.0 copy.127
  171.2 3.0 fusion.45
  177.2 1.5 constant_dynamic-slice_fusion.5
  181.1 2.5 fusion.44
  183.6 2.0 copy.127
  186.2 3.0 fusion.45
  192.1 1.6 constant_dynamic-slice_fusion.5
  196.1 2.5 fusion.44
  198.6 2.0 copy.127
  201.2 3.0 fusion.45
  207.1 51.2 %all-reduce.3.cloned.1.call-done = bf16[2,32,16,2560]{3,2,1,0:T(8,128)(2,1)} async-done(((bf16[2,32,16,2560]{3,2,1,0:T(8,128)(2,1)}), bf16[2,32,16,2560]{3,2,1,0:T(8,128)(2,1)}) %all-reduce.3.cloned.1.call-update) | async-done | bytes 5242896 | tf_op jit(solution)/shard_map/psum | solution.py:42
  258.3 74.7 %while.39 = (s32[]{:T(128)}, f32[20,128]{1,0:T(8,128)S(1)}, f32[20,128]{1,0:T(8,128)S(1)}, f32[128,20,128]{0,2,1:T(8,128)}, bf16[2,32,16,2560]{3,2,1,0:T(8,128)(...) while((s32[]{:T(128)}, f32[20,128]{1,0:T(8,128)S(1)}, ...), condition=%wide.region_9.10_spmd.clone, body=%wide.region_6.9_spmd.clone.sunk | while | flops 43929608 | bytes 16578803 | solution.py:180
  258.3 1.2 constant_dynamic-slice_fusion.6
  259.6 1.5 fusion.48
  263.0 1.1 constant_dynamic-slice_fusion.6
  264.3 1.5 fusion.48
  267.7 1.1 constant_dynamic-slice_fusion.6
  268.9 1.5 fusion.48
  272.3 1.1 constant_dynamic-slice_fusion.6
  273.6 1.5 fusion.48
  277.0 1.1 constant_dynamic-slice_fusion.6
  278.3 1.5 fusion.48
  281.7 1.1 constant_dynamic-slice_fusion.6
  282.9 1.5 fusion.48
  286.3 1.1 constant_dynamic-slice_fusion.6
  287.6 1.5 fusion.48
  291.0 1.1 constant_dynamic-slice_fusion.6
  292.3 1.5 fusion.48
  295.7 1.1 constant_dynamic-slice_fusion.6
  296.9 1.5 fusion.48
  300.3 1.1 constant_dynamic-slice_fusion.6
  301.6 1.5 fusion.48
  305.0 1.1 constant_dynamic-slice_fusion.6
  306.2 1.5 fusion.48
  309.7 1.1 constant_dynamic-slice_fusion.6
  310.9 1.5 fusion.48
  315.6 1.5 fusion.48
  320.2 1.5 fusion.48
  324.9 1.5 fusion.48
  329.6 1.5 fusion.48
  333.0 1.7 divide_convert_fusion
  (338 shorter events, 67.6 us)
Async XLA Ops:
  6.5 45.5 %copy-start = (bf16[4,2,16,2560]{3,2,1,0:T(8,128)(2,1)S(1)}, bf16[4,2,16,2560]{3,2,1,0:T(8,128)(2,1)}, u32[]{:S(2)}) copy-start(bf16[4,2,16,2560]{3,2,1,0:T(8,128)(2,1)} %param.9) | copy-start | bytes 1966084
  6.5 2.7 copy-start.5
  6.5 2.7 copy-start.6
  6.5 121.5 %all-gather.3.cloned.1.call-start = ((), (), s32[]{:S(2)}) async-start(), calls=%async_computation.1 | async-start | bytes 5570560 | tf_op jit(solution)/shard_map/all_gather | solution.py:155
  9.1 249.1 %all-reduce.3.cloned.1.call-start = ((), (), s32[]{:S(2)}) async-start(), calls=%async_computation | async-start | bytes 10485760 | tf_op jit(solution)/shard_map/psum | solution.py:42
  9.3 41.9 %copy-start.8 = (s32[1,1,2,18]{3,2,1,0:T(2,128)S(1)}, s32[1,1,2,18]{3,2,1,0:T(2,128)}, u32[]{:S(2)}) copy-start(s32[1,1,2,18]{3,2,1,0:T(2,128)} %param.12) | copy-start | bytes 436
  9.4 31.8 %collective-permute-start = (bf16[2,4,2,16,2560]{4,3,2,0,1:T(8,128)(2,1)S(1)}, bf16[2,4,2,16,2560]{4,3,2,0,1:T(8,128)(2,1)S(1)}, u32[]{:S(2)}, u32[]{:S(2)}) collective-permute-start(bf16[2,4,2,16,2560]{4,3,2,0,1:T(8,128)(2,1)S(1)} %pad_maximum_fusion.2), channel_id=1, source_target_pairs={{0,16},{16,32},{32,48},{48,64},{64,80},{80,96},{96,112},{1,17},{17... | collective-permute-start | bytes 3932168 | tf_op jit(solution)/shard_map/ppermute | solution.py:20
  42.9 48.0 %collective-permute-start.1 = (bf16[2,8,2,16,2560]{4,3,2,0,1:T(8,128)(2,1)}, bf16[2,8,2,16,2560]{4,3,2,0,1:T(8,128)(2,1)}, u32[]{:S(2)}, u32[]{:S(2)}) collective-permute-start(bf16[2,8,2,16,2560]{4,3,2,0,1:T(8,128)(2,1)} %maximum_maximum_fusion), channel_id=1, source_target_pairs={{0,1},{1,2},{2,3},{3,4},{4,5},{5,6},{6,7},{7,8},{8,9},{9,10},{10,1... | collective-permute-start | bytes 7864328 | tf_op jit(solution)/shard_map/ppermute | solution.py:31
  49.0 72.7 %collective-permute-start.2 = (bf16[2,8,2,16,2560]{4,3,2,0,1:T(8,128)(2,1)}, bf16[2,8,2,16,2560]{4,3,2,0,1:T(8,128)(2,1)}, u32[]{:S(2)}, u32[]{:S(2)}) collective-permute-start(bf16[2,8,2,16,2560]{4,3,2,0,1:T(8,128)(2,1)} %maximum_maximum_fusion), channel_id=1, source_target_pairs={{1,0},{2,1},{3,2},{4,3},{5,4},{6,5},{7,6},{8,7},{9,8},{10,9},{11,1... | collective-permute-start | bytes 7864328 | tf_op jit(solution)/shard_map/ppermute | solution.py:33
  141.0 3.4 copy-start.2
  156.3 3.0 copy-start.2
  171.2 3.0 copy-start.2
  186.2 3.0 copy-start.2
  201.1 3.0 copy-start.2
  258.3 74.7 %copy-start.7 = (f32[128,20,128]{0,2,1:T(8,128)S(1)}, f32[128,20,128]{0,2,1:T(8,128)}, u32[]{:S(2)}) copy-start(f32[128,20,128]{0,2,1:T(8,128)} %get-tuple-element.295) | copy-start | bytes 3932164
  258.3 3.1 copy-start.3
  261.9 1.1 copy-start.4
  263.0 3.0 copy-start.3
  266.6 1.1 copy-start.4
  267.7 3.0 copy-start.3
  271.3 1.1 copy-start.4
  272.3 3.0 copy-start.3
  275.9 1.1 copy-start.4
  277.0 3.0 copy-start.3
  280.6 1.1 copy-start.4
  281.7 3.0 copy-start.3
  285.3 1.1 copy-start.4
  286.3 3.0 copy-start.3
  289.9 1.1 copy-start.4
  291.0 3.0 copy-start.3
  294.6 1.1 copy-start.4
  295.7 3.0 copy-start.3
  299.3 1.1 copy-start.4
  300.3 3.0 copy-start.3
  303.9 1.1 copy-start.4
  305.0 3.0 copy-start.3
  308.6 1.1 copy-start.4
  309.7 3.0 copy-start.3
  313.3 1.1 copy-start.4
  314.3 3.0 copy-start.3
  317.9 1.1 copy-start.4
  319.0 3.0 copy-start.3
  322.6 1.1 copy-start.4
  323.7 3.0 copy-start.3
  327.3 1.1 copy-start.4
  328.3 3.0 copy-start.3
  331.9 1.1 copy-start.4
  333.0 3.4 copy-start.1
Sparse Core Ops, SparseCore 0:
  9.8 77.6 all-gather.2
  130.8 127.4 all-reduce.2
where the time goes:
time: 344 us; the launch traced here: 343 us
  waiting for transfers between devices  146 us (42%)
  local copies, waits for them, and re-layouts  91.8 us (27%)
  matrix products  52.2 us (15%)
  other arithmetic  24.2 us (7%)
  between operations  14.4 us (4%)
  starting transfers between devices  12.5 us (4%)
    psum x1, waiting for transfers between devices, from_root(): return lax.psum(jnp.where(mine, x, jnp.zeros_like(x)), axis)  51.2 us
    ppermute x1, waiting for transfers between devices, with_halo(): lax.ppermute(tail, axis, [(i, (i + 1) % count) for i in range(ends)])  36.8 us
    ppermute x1, waiting for transfers between devices, with_halo(): lax.ppermute(head, axis, [((i + 1) % count, i) for i in range(ends)])  30.7 us
    ppermute x1, waiting for transfers between devices, from_behind(): lax.ppermute(value, axis, [(source, source + steps) for source in range(f...  27.3 us
    dot_general x16, matrix products, band_step(): jnp.einsum('qhd,khd->hqk', q_flat, key_block, preferred_element_type=jnp....  24.7 us
    slice x16, local copies, waits for them, and re-layouts, band_step(): val_block = block_rows[1].reshape(row_count * col_count, head_count, HD)  18 us
    while x90, local copies, waits for them, and re-layouts  16.8 us
    slice x10, local copies, waits for them, and re-layouts, head_step(): shifted[1]  15.4 us
  transfers between devices with their start and end apart: 5, of which 4 were waited for; matrix products, arithmetic and copies ran while one was open for 25% of the time, Pallas kernels for 0%

commit v1 on v0

v1 whole, which is shorter than its diff:
```python
import math

import jax
import jax.numpy as jnp
from jax import lax
from jax.experimental import pallas as pl
from jax.experimental.pallas import tpu as pltpu
from jax.sharding import PartitionSpec as P

H = 20
HD = 128
TF = 4
TC = 8
COLS = 16
E = H * HD
TOK = 128
SINK = 32
HALF = E // 2
CHUNK = 2 * HD
CHUNKS = E // CHUNK
EARLY = 3
MASKED = -1e30
SCALE = math.log2(math.e) / math.sqrt(HD)
MESH = pl.DeviceIdType.MESH
F32, BF16 = jnp.float32, jnp.bfloat16


def attend(q_hbm, k_hbm, v_hbm, mask_ref, sink_ref, out_ref,
           qbuf, kbuf, vbuf, flags, bias, sel, zin, zsum, xin, skv, ones, part, back, ours, stats, theirs,
           local_sem, halo_s, halo_r, core_s, core_r, q_s, q_r, flag_s, flag_r, z_s, z_r, lo_s, lo_r,
           x_s, x_r, y_s, y_r, f_s, f_r, o_s, o_r, st_s, st_r):
    tm, h = lax.axis_index("tm"), lax.axis_index("height")
    lo, z, y, hi, c = tm // 4, tm % 4, h // 4, (h // 2) % 2, h % 2
    x = hi * 2 + lo
    parity = tm % 2

    def at(x, y, z, c):
        x, y, z = (x + 4) % 4, (y + 4) % 4, (z + 4) % 4
        return ((x % 2) * 4 + z, y * 4 + (x // 2) * 2 + c)

    partner = at(x, y, z, 1 - c)
    beyond = (tm, (h + 2 * c - 1 + 16) % 16)
    earlier, later = ((tm + 7) % 8, h), ((tm + 1) % 8, h)
    z_mates = [at(x, y, z + d, c) for d in (1, -1, 2)]
    x_mates = [at(x + d, y, z, c) for d in (1, -1, 2)]
    y_mates = [at(x, y + d, z, c) for d in (1, -1, 2)]
    lo_mate = at(hi * 2 + 1 - lo, y, z, c)

    def remote(src, dst, send, recv, device):
        return pltpu.make_async_remote_copy(src, dst, send, recv, device_id=device, device_id_type=MESH)

    local = [
        pltpu.make_async_copy(k_hbm, kbuf.at[pl.ds(TOK, TOK)], local_sem.at[0]),
        pltpu.make_async_copy(v_hbm, vbuf.at[pl.ds(TOK, TOK)], local_sem.at[1]),
        pltpu.make_async_copy(q_hbm, qbuf.at[pl.ds(0, TOK)], local_sem.at[2]),
    ]
    for copy in local:
        copy.start()
    barrier = pltpu.get_barrier_semaphore()
    friends = [partner, beyond, earlier, later, *z_mates, *x_mates, *y_mates]
    for friend in friends:
        pl.semaphore_signal(barrier, inc=1, device_id=friend, device_id_type=MESH)

    flags[0] = jnp.zeros((8, 128), F32)
    flags[0, 0:2, 0:18] = mask_ref[...].astype(F32)
    stats[...] = jnp.zeros_like(stats)
    ones[...] = jnp.ones_like(ones)
    for copy in local:
        copy.wait()

    frame = (sink_ref[0] - tm * TF).astype(F32)
    for i, buf in enumerate((kbuf, vbuf)):
        tokens = 0.0
        for f in range(TF):
            mine = jnp.where(frame == f, 1.0, 0.0).astype(F32)
            tokens = tokens + buf[TOK + f * SINK:TOK + (f + 1) * SINK, :].astype(F32) * mine
        tokens = tokens.astype(BF16)
        sel[0, i] = tokens[:, :HALF]
        sel[1, i] = tokens[:, HALF:]
    pl.semaphore_wait(barrier, len(friends))

    def place(step, par):
        half = jnp.where(step < CHUNKS // 2, 1 - par, par)
        return pl.multiple_of(half * HALF + (step % (CHUNKS // 2)) * CHUNK, CHUNK)

    def halo(step):
        lanes = pl.ds(place(step, parity), CHUNK)
        return [
            remote(buf.at[pl.ds(TOK, TOK), lanes], buf.at[pl.ds(2 * TOK, TOK), lanes],
                   halo_s.at[i, step], halo_r.at[i, step], beyond)
            for i, buf in enumerate((kbuf, vbuf))
        ]

    def q_out(step, par):
        lanes = pl.ds(place(step, par), CHUNK)
        return remote(qbuf.at[pl.ds(0, TOK), lanes], qbuf.at[pl.ds(TOK, TOK), lanes],
                      q_s.at[step], q_r.at[step], earlier)

    def send(step):
        for copy in halo(step):
            copy.start()
        q_out(step, 1 - parity).start()

    def o_back(step):
        lanes = pl.ds(place(step, parity), CHUNK)
        return remote(part.at[:, lanes], back.at[:, lanes], o_s.at[step], o_r.at[step], later)

    to_z = [
        remote(sel.at[half], zin.at[i], z_s.at[i], z_r.at[i], mate)
        for i, (half, mate) in enumerate(zip((1 - parity, 1 - parity, parity), z_mates))
    ]
    flag_copy = remote(flags.at[0], flags.at[1], flag_s, flag_r, earlier)
    core_copies = [
        remote(buf.at[pl.ds(TOK, TOK)], buf.at[pl.ds(0, TOK)], core_s.at[i], core_r.at[i], partner)
        for i, buf in enumerate((kbuf, vbuf))
    ]
    for copy in to_z:
        copy.start()
    flag_copy.start()
    for step in range(EARLY):
        send(step)
    for copy in core_copies:
        copy.start()

    def make_bias():
        lane = lax.broadcasted_iota(jnp.int32, (1, TOK), 1)
        key_first = (lane % COLS) < TC
        rows = lax.broadcasted_iota(jnp.int32, (TOK, TOK), 0)
        query_first = (rows % COLS) < TC
        at_zero = (1 - c).astype(F32)
        at_one = c.astype(F32)
        band_ok = jnp.where((h + 2 * c - 1 >= 0) & (h + 2 * c - 1 < 16), 1.0, 0.0).astype(F32)
        time_ok = jnp.where(tm < 7, 1.0, 0.0).astype(F32)
        for which, base in ((0, 9), (1, 0)):
            def flag(cq, dh, dw):
                code = base + dh * 3 + dw
                return flags[which, cq:cq + 1, code:code + 1]

            for slot in range(3):
                lines = []
                for cq in range(2):
                    pair = []
                    for ck in range(2):
                        dw = ck - cq + 1
                        if slot == 1:
                            value = flag(cq, 1, dw)
                            if which == 0 and dw == 1:
                                value = jnp.ones_like(value)
                        else:
                            first, second = (2, 0) if slot == 0 else (0, 2)
                            value = flag(cq, first, dw) * at_zero + flag(cq, second, dw) * at_one
                        if slot == 2:
                            value = value * band_ok
                        if which == 1:
                            value = value * time_ok
                        pair.append(value)
                    lines.append(jnp.where(key_first, pair[0], pair[1]))
                allowed = jnp.where(query_first, lines[0], lines[1])
                bias[which * TOK:(which + 1) * TOK, slot * TOK:(slot + 1) * TOK] = jnp.where(
                    allowed > 0.5, 0.0, MASKED
                )

    def head(lane, sink_lane, number):
        lanes = pl.ds(lane, HD)
        q = qbuf[:, lanes]
        contract = (((1,), (1,)), ((), ()))
        scores = lax.dot_general(q, kbuf[:, lanes], contract, preferred_element_type=F32) + bias[...]
        top = jnp.max(scores, axis=1, keepdims=True)
        if sink_lane is not None:
            lines = pl.ds(sink_lane, HD)
            sink_k = skv[:, :, 0, :, lines].reshape(512, HD)
            sink_v = skv[:, :, 1, :, lines].reshape(512, HD)
            sink_scores = lax.dot_general(q, sink_k, contract, preferred_element_type=F32)
            top = jnp.maximum(top, jnp.max(sink_scores, axis=1, keepdims=True))
        probs = jnp.exp2((scores - top) * SCALE).astype(BF16)
        vals = jnp.concatenate([vbuf[:, lanes], ones[0:3 * TOK]], axis=1)
        total = jnp.dot(probs, vals, preferred_element_type=F32)
        if sink_lane is not None:
            sink_probs = jnp.exp2((sink_scores - top) * SCALE).astype(BF16)
            vals = jnp.concatenate([sink_v, ones[...]], axis=1)
            total = total + jnp.dot(sink_probs, vals, preferred_element_type=F32)
        weighted, norm = total[:, :HD], total[:, HD:]
        ours[:, lanes] = weighted[:TOK]
        part[:, lanes] = (weighted[TOK:] / norm[TOK:]).astype(BF16)
        spot = lax.broadcasted_iota(jnp.int32, (2 * TOK, 128), 1)
        stats[...] = jnp.where(spot == number, top, jnp.where(spot == number + 64, norm, stats[...]))

    def chunk(step, with_sink):
        for copy in halo(step):
            copy.wait_recv()
        q_out(step, 1 - parity).wait_recv()
        lane = place(step, parity)
        for i in range(CHUNK // HD):
            sink_lane = None
            if with_sink:
                sink_lane = pl.multiple_of((step % (CHUNKS // 2)) * CHUNK + i * HD, HD)
            head(pl.multiple_of(lane + i * HD, HD), sink_lane, lane // HD + i)
        o_back(step).start()

    make_sum = [sel.at[parity], zin.at[0], zin.at[1], zin.at[2]]
    for copy in to_z:
        copy.wait_recv()
    zsum[...] = sum(ref[...].astype(F32) for ref in make_sum).astype(BF16)
    lo_copy = remote(zsum.at[1 - lo], xin, lo_s, lo_r, lo_mate)
    lo_copy.start()
    send(EARLY)
    flag_copy.wait_recv()
    make_bias()
    for copy in core_copies:
        copy.wait_recv()
    chunk(0, False)
    lo_copy.wait_recv()
    own = skv.at[0, 0, lo, pl.ds(pl.multiple_of(hi * SINK, SINK), SINK)]
    own[...] = (zsum[lo].astype(F32) + xin[...].astype(F32)).astype(BF16)
    to_x = [remote(own, own, x_s.at[i], x_r.at[i], mate) for i, mate in enumerate(x_mates)]
    for copy in to_x:
        copy.start()
    for step in range(EARLY + 1, CHUNKS):
        send(step)
    chunk(1, False)
    chunk(2, False)

    def place_of(xx):
        xx = (xx + 4) % 4
        return skv.at[0, 0, xx % 2, pl.ds(pl.multiple_of((xx // 2) * SINK, SINK), SINK)]

    for i, d in enumerate((-1, 1, 2)):
        remote(own, place_of(x + d), x_s.at[i], x_r.at[i], x_mates[i]).wait_recv()
    to_y = [remote(skv.at[0, 0], skv.at[i + 1, 0], y_s.at[i], y_r.at[i], mate) for i, mate in enumerate(y_mates)]
    across = [remote(skv.at[i, 0], skv.at[i, 1], f_s.at[i], f_r.at[i], partner) for i in range(4)]
    for copy in to_y:
        copy.start()
    across[0].start()
    chunk(3, False)
    chunk(4, False)
    for i in range(3):
        to_y[i].wait_recv()
        across[i + 1].start()
    for copy in across:
        copy.wait_recv()

    def sink_chunk(step, carry):
        chunk(step, True)
        return carry

    lax.fori_loop(CHUNKS // 2, CHUNKS, sink_chunk, 0)
    st_copy = remote(stats.at[pl.ds(TOK, TOK)], theirs, st_s, st_r, later)
    st_copy.start()
    st_copy.wait_recv()
    for step in range(CHUNKS):
        remote(part.at[:, pl.ds(0, CHUNK)], back.at[:, pl.ds(place(step, 1 - parity), CHUNK)],
               o_s.at[step], o_r.at[step], later).wait_recv()

    top_a, top_b = stats[0:TOK], theirs[...]
    norm_a, norm_b = pltpu.roll(top_a, 64, 1), pltpu.roll(top_b, 64, 1)
    top = jnp.maximum(top_a, top_b)
    weight_a = jnp.exp2((top_a - top) * SCALE)
    weight_b = jnp.exp2((top_b - top) * SCALE) * norm_b
    inverse = 1.0 / (weight_a * norm_a + weight_b)
    weight_a, weight_b = weight_a * inverse, weight_b * inverse
    for i in range(H):
        lanes = slice(i * HD, (i + 1) * HD)
        out_ref[:, lanes] = (
            weight_a[:, i:i + 1] * ours[:, lanes] + weight_b[:, i:i + 1] * back[:, lanes].astype(F32)
        ).astype(BF16)

    for copy in [*to_z, flag_copy, *core_copies, lo_copy, *to_x, *to_y, *across, st_copy]:
        copy.wait_send()
    for step in range(CHUNKS):
        for copy in halo(step):
            copy.wait_send()
        q_out(step, 1 - parity).wait_send()
        o_back(step).wait_send()


def shards(queries, keys, values, tile_mask, sink_frame):
    any_spec, vmem, smem = (pl.BlockSpec(memory_space=space) for space in (pl.ANY, pltpu.VMEM, pltpu.SMEM))
    sems = pltpu.SemaphoreType.DMA
    out = pl.pallas_call(
        attend,
        out_shape=jax.ShapeDtypeStruct((TOK, E), BF16),
        in_specs=[any_spec, any_spec, any_spec, vmem, smem],
        out_specs=vmem,
        scratch_shapes=[
            pltpu.VMEM((2 * TOK, E), BF16),
            pltpu.VMEM((3 * TOK, E), BF16),
            pltpu.VMEM((3 * TOK, E), BF16),
            pltpu.VMEM((2, 8, 128), F32),
            pltpu.VMEM((2 * TOK, 3 * TOK), F32),
            pltpu.VMEM((2, 2, SINK, HALF), BF16),
            pltpu.VMEM((3, 2, SINK, HALF), BF16),
            pltpu.VMEM((2, SINK, HALF), BF16),
            pltpu.VMEM((SINK, HALF), BF16),
            pltpu.VMEM((4, 2, 2, 2 * SINK, HALF), BF16),
            pltpu.VMEM((4 * TOK, HD), BF16),
            pltpu.VMEM((TOK, E), BF16),
            pltpu.VMEM((TOK, E), BF16),
            pltpu.VMEM((TOK, E), F32),
            pltpu.VMEM((2 * TOK, 128), F32),
            pltpu.VMEM((TOK, 128), F32),
            sems((3,)),
            sems((2, CHUNKS)), sems((2, CHUNKS)),
            sems((2,)), sems((2,)),
            sems((CHUNKS,)), sems((CHUNKS,)),
            sems, sems,
            sems((3,)), sems((3,)),
            sems, sems,
            sems((3,)), sems((3,)),
            sems((3,)), sems((3,)),
            sems((4,)), sems((4,)),
            sems((CHUNKS,)), sems((CHUNKS,)),
            sems, sems,
        ],
        compiler_params=pltpu.CompilerParams(
            collective_id=0, has_side_effects=True, vmem_limit_bytes=48 * 2**20
        ),
        cost_estimate=pl.CostEstimate(flops=2 * 10**9, bytes_accessed=3 * 10**6, transcendentals=4 * 10**6),
    )(
        queries.reshape(TOK, E), keys.reshape(TOK, E), values.reshape(TOK, E),
        tile_mask.reshape(2, 18), sink_frame,
    )
    return out.reshape(queries.shape)


def solution(mesh):
    spec = P("tm", "height", None, None)
    return jax.shard_map(
        shards,
        mesh=mesh,
        in_specs=(spec, spec, spec, spec, P()),
        out_specs=spec,
        check_vma=False,
    )
```

time: 344 us -> 74 us (0.22)
  waiting for transfers between devices: 146 us -> 0 us
  local copies, waits for them, and re-layouts: 91.8 us -> 4.77 us
  Pallas kernels: 0 us -> 68 us
  matrix products: 52.2 us -> 0 us
  other arithmetic: 24.2 us -> 0 us
  between operations: 14.4 us -> 0.67 us
  starting transfers between devices: 12.5 us -> 0 us
    ppermute x3 -> x0, waiting for transfers between devices: 94.9 us -> none  [the longest x1 36.8 us: with_halo(): lax.ppermute(tail, axis, [(i, (i + 1) % count) for i in range(ends)])]
    pallas_call x0 -> x1, Pallas kernels: none -> 68 us  [shards(): pl.pallas_call(attend, out_shape=jax.ShapeDtypeStruct((TOK, E), BF16), in...]
    dot_general x42 -> x0, matrix products: 52.2 us -> none  [the longest x16 24.7 us: band_step(): jnp.einsum('qhd,khd->hqk', q_flat, key_block, preferred_element_type=jnp....]
    psum x1 -> x0, waiting for transfers between devices: 51.2 us -> none  [from_root(): return lax.psum(jnp.where(mine, x, jnp.zeros_like(x)), axis)]
    slice x46 -> x0, local copies, waits for them, and re-layouts: 45.4 us -> none  [the longest x16 18 us: band_step(): val_block = block_rows[1].reshape(row_count * col_count, head_count, HD)]
    while x90 -> x0, local copies, waits for them, and re-layouts: 16.8 us -> none
    ppermute x3 -> x0, starting transfers between devices: 12.4 us -> none  [the longest x1 6.07 us: with_halo(): lax.ppermute(tail, axis, [(i, (i + 1) % count) for i in range(ends)])]
    dynamic_slice x10 -> x0, local copies, waits for them, and re-layouts: 8.54 us -> none  [head_step(): win_part = lax.dynamic_slice_in_dim(window, offset * HD, group_size * HD, 4)]
  transfers between devices with their start and end apart: 5 -> 0, of which waited for: 4 -> 0; matrix products, arithmetic and copies ran while one was open for 25% -> 0% of each run, Pallas kernels for 0% -> 0%
where the time goes in v1:
time: 74 us; the launch traced here: 73.4 us
  Pallas kernels  68 us (92%)
  local copies, waits for them, and re-layouts  4.77 us (6%)
    pallas_call x1, Pallas kernels, shards(): pl.pallas_call(attend, out_shape=jax.ShapeDtypeStruct((TOK, E), BF16), in...  68 us
    unnamed x9, local copies, waits for them, and re-layouts  4.77 us

profile of v1, /device:TPU:1, one launch (start us, length us, event | category | flops | bytes accessed | tf_op | source)
XLA Modules:
  0.0 73.4 jit_solution(1402598127877208412)
XLA Ops:
  0.7 0.0 copy-start.3
  0.7 0.7 copy-done.3
  1.3 0.0 copy-start
  1.3 1.1 %copy-done = bf16[4,2,16,2560]{3,2,1,0:T(8,128)(2,1)S(1)} copy-done((bf16[4,2,16,2560]{3,2,1,0:T(8,128)(2,1)S(1)}, bf16[4,2,16,2560]{3,2,1,0:T(8,128)(2,1)}, u32[]{:S(2)}) %copy-start) | copy-done | bytes 655384
  2.4 0.0 copy-start.1
  2.4 1.1 %copy-done.1 = bf16[4,2,16,2560]{3,2,1,0:T(8,128)(2,1)S(1)} copy-done((bf16[4,2,16,2560]{3,2,1,0:T(8,128)(2,1)S(1)}, bf16[4,2,16,2560]{3,2,1,0:T(8,128)(2,1)}, u32[]{:S(2)}) %copy-start.1) | copy-done | bytes 655384
  3.5 0.0 copy-start.2
  3.5 1.1 %copy-done.2 = bf16[4,2,16,2560]{3,2,1,0:T(8,128)(2,1)S(1)} copy-done((bf16[4,2,16,2560]{3,2,1,0:T(8,128)(2,1)S(1)}, bf16[4,2,16,2560]{3,2,1,0:T(8,128)(2,1)}, u32[]{:S(2)}) %copy-start.2) | copy-done | bytes 655384
  4.6 68.0 %shard_map.55 = bf16[128,2560]{1,0:T(8,128)(2,1)S(1)} custom-call(bf16[128,2560]{1,0:T(8,128)(2,1)S(1)} %bitcast.6, bf16[128,2560]{1,0:T(8,128)(2,1)S(1)} %bitcast.7, bf16[128,2560]{1,0:T(8,128)(2,1)S(1)} %bitcast.8, s32[2,18]{1,0:T(2,128)S(1)} %bitcast.9, s32[1]{0:T(128)S(6)} %copy.7.sink_ref), custom_call_target="tpu_custom_call" | custom-call | flops 2000000000 | bytes 3000000 | tf_op jit(solution)/shard_map/pallas_call | solution.py:279
  72.6 0.8 %copy.8 = bf16[4,2,16,2560]{3,2,1,0:T(8,128)(2,1)} copy(bf16[4,2,16,2560]{3,2,1,0:T(8,128)(2,1)S(1)} %bitcast.5) | data formatting | bytes 1310720
Async XLA Ops:
  0.7 0.7 copy-start.3
  1.3 1.1 %copy-start = (bf16[4,2,16,2560]{3,2,1,0:T(8,128)(2,1)S(1)}, bf16[4,2,16,2560]{3,2,1,0:T(8,128)(2,1)}, u32[]{:S(2)}) copy-start(bf16[4,2,16,2560]{3,2,1,0:T(8,128)(2,1)} %param.5) | copy-start | bytes 1966084
  2.4 1.1 %copy-start.1 = (bf16[4,2,16,2560]{3,2,1,0:T(8,128)(2,1)S(1)}, bf16[4,2,16,2560]{3,2,1,0:T(8,128)(2,1)}, u32[]{:S(2)}) copy-start(bf16[4,2,16,2560]{3,2,1,0:T(8,128)(2,1)} %param.6) | copy-start | bytes 1966084
  3.5 1.1 %copy-start.2 = (bf16[4,2,16,2560]{3,2,1,0:T(8,128)(2,1)S(1)}, bf16[4,2,16,2560]{3,2,1,0:T(8,128)(2,1)}, u32[]{:S(2)}) copy-start(bf16[4,2,16,2560]{3,2,1,0:T(8,128)(2,1)} %param.7) | copy-start | bytes 1966084

commit v2 on v1

v2 whole, which is shorter than its diff:
```python
import math

import jax
import jax.numpy as jnp
from jax import lax
from jax.experimental import pallas as pl
from jax.experimental.pallas import tpu as pltpu
from jax.sharding import PartitionSpec as P

H = 20
HD = 128
TF = 4
TC = 8
COLS = 16
E = H * HD
TOK = 128
SINK = 32
G = 5
GE = G * HD
BANDS = 4
EARLY = 2
MASKED = -1e30
SCALE = math.log2(math.e) / math.sqrt(HD)
MESH = pl.DeviceIdType.MESH
F32, BF16 = jnp.float32, jnp.bfloat16


def attend(q_hbm, k_hbm, v_hbm, mask_hbm, sink_ref, out_ref,
           mask_ref, qsrc, kvsrc, flags, flags_in, flags_next, bias, sel, xin, zown, zin, skv, ones,
           q_in, q_next, kv, part, back, stat, stat_in, ours, our_top, our_sum, outs,
           local_sem, fx_s, fx_r, fz_s, fz_r, kv_s, kv_r, q_s, q_r, y_s, y_r, n_s, n_r, b_s, b_r, st_s, st_r,
           sx_s, sx_r, sz_s, sz_r, sy_s, sy_r, sc_s, sc_r, o_s, o_r):
    tm, h = lax.axis_index("tm"), lax.axis_index("height")
    lo, z, y, hi, c = tm // 4, tm % 4, h // 4, (h // 2) % 2, h % 2
    x = hi * 2 + lo
    time = z + 4 * c

    def at(x, y, z, c):
        x, y, z = (x + 4) % 4, (y + 4) % 4, (z + 4) % 4
        return ((x % 2) * 4 + z, y * 4 + (x // 2) * 2 + c)

    def at_time(t):
        t = (t + 8) % 8
        return at(x, y, t % 4, t // 4)

    partner = at(x, y, z, 1 - c)
    earlier, later = at_time(time - 1), at_time(time + 1)
    steps = (1, -1, 2)
    y_mates = [at(x, y + d, z, c) for d in steps]
    z_mates = [at(x, y, z + d, c) for d in steps]

    def remote(src, dst, send, recv, device):
        return pltpu.make_async_remote_copy(src, dst, send, recv, device_id=device, device_id_type=MESH)

    local = [
        pltpu.make_async_copy(k_hbm, kvsrc.at[0], local_sem.at[0]),
        pltpu.make_async_copy(v_hbm, kvsrc.at[1], local_sem.at[1]),
        pltpu.make_async_copy(q_hbm, qsrc, local_sem.at[2]),
        pltpu.make_async_copy(mask_hbm, mask_ref, local_sem.at[3]),
    ]
    for copy in local:
        copy.start()
    barrier = pltpu.get_barrier_semaphore()
    friends = [at(x + d, y, z, core) for d in steps for core in range(2)]
    friends += [partner, earlier, later, *y_mates, *z_mates]
    for friend in friends:
        pl.semaphore_signal(barrier, inc=1, device_id=friend, device_id_type=MESH)
    ones[...] = jnp.ones_like(ones)
    stat[...] = jnp.zeros_like(stat)
    flags[...] = jnp.zeros_like(flags)
    for copy in local:
        copy.wait()
    flags[0:2, 0:18] = mask_ref[...].astype(F32)

    frame = (sink_ref[0] - tm * TF).astype(F32)
    for i in range(2):
        tokens = 0.0
        for f in range(TF):
            mine = jnp.where(frame == f, 1.0, 0.0).astype(F32)
            tokens = tokens + kvsrc[i, f * SINK:(f + 1) * SINK, :].astype(F32) * mine
        sel[i] = tokens.astype(BF16)
    pl.semaphore_wait(barrier, len(friends))

    def own_lanes(xx):
        return pl.ds(pl.multiple_of(((xx + 4) % 4) * GE, HD), GE)

    band = hi * 2 + c

    class Either:
        def __init__(self, src, dst, send, recv, device, here):
            self.far = lambda: remote(src, dst, send, recv, device)
            self.near = lambda: pltpu.make_async_copy(src, dst, recv)
            self.here = here

        def start(self):
            pl.when(self.here)(lambda: self.near().start())
            pl.when(jnp.logical_not(self.here))(lambda: self.far().start())

        def wait_send(self):
            pl.when(jnp.logical_not(self.here))(lambda: self.far().wait_send())

        def wait_recv(self):
            self.far().wait_recv()

    def fan(make):
        copies = [make(i, x + d, at(x + d, y, z, lo), remote) for i, d in enumerate(steps)]
        here = c == lo

        def either(*args):
            return Either(*args, here)

        return copies + [make(3, x, partner, either)]

    def deal(g):
        def lanes(xx):
            return pl.ds(pl.multiple_of(((xx + 4) % 4) * GE + g * HD, HD), HD)

        def of_kv(i, xx, device, how):
            return how(kvsrc.at[:, :, lanes(xx)], kv.at[g, :, band + 1], kv_s.at[g, i], kv_r.at[g, band], device)

        def of_q(i, xx, device, how):
            return how(qsrc.at[:, lanes(xx)], q_in.at[g, band], q_s.at[g, i], q_r.at[g, band], device)

        return fan(of_kv) + fan(of_q)

    def dealt(g):
        copies = [remote(kvsrc.at[:, :, pl.ds(0, HD)], kv.at[g, :, b + 1], kv_s.at[g, 0], kv_r.at[g, b], partner)
                  for b in range(BANDS)]
        return copies + [remote(qsrc.at[:, pl.ds(0, HD)], q_in.at[g, b], q_s.at[g, 0], q_r.at[g, b], partner)
                         for b in range(BANDS)]

    def edges(g):
        return [
            remote(kv.at[g, :, 4], kv.at[g, :, 0], y_s.at[g, 0], y_r.at[g, 0], y_mates[0]),
            remote(kv.at[g, :, 1], kv.at[g, :, 5], y_s.at[g, 1], y_r.at[g, 1], y_mates[1]),
        ]

    def ask(g):
        return remote(q_in.at[g], q_next.at[g], n_s.at[g], n_r.at[g], earlier)

    def answer(g):
        return [
            remote(part.at[g], back.at[g], b_s.at[g], b_r.at[g], later),
            remote(stat.at[g], stat_in.at[g], st_s.at[g], st_r.at[g], later),
        ]

    def out_copies(g):
        copies = []
        for b in range(BANDS):
            xx, core = (b // 2) * 2 + c, b % 2
            copies.append(Either(
                outs.at[g, b], out_ref.at[:, pl.ds(pl.multiple_of(x * GE + g * HD, HD), HD)],
                o_s.at[g, b], o_r.at[g, x], at(xx, y, z, core), (xx == x) & (c == core),
            ))
        return copies

    flag_copies = fan(lambda i, xx, device, how: how(flags, flags_in.at[band], fx_s.at[i], fx_r.at[band], device))
    flag_next = remote(flags_in, flags_next, fz_s, fz_r, earlier)
    sink_x = [
        remote(sel.at[:, :, own_lanes(x + d)], xin.at[x], sx_s.at[i], sx_r.at[i], at(x + d, y, z, c))
        for i, d in enumerate(steps)
    ]
    sink_z = [remote(zown, zin.at[i], sz_s.at[i], sz_r.at[i], mate) for i, mate in enumerate(z_mates)]
    sink_y = [remote(skv.at[0, 0], skv.at[i + 1, 0], sy_s.at[i], sy_r.at[i], mate) for i, mate in enumerate(y_mates)]
    sink_c = [remote(skv.at[i, 0], skv.at[i, 1], sc_s.at[i], sc_r.at[i], partner) for i in range(4)]

    def start(copies):
        for copy in copies:
            copy.start()

    def landed(copies):
        for copy in copies:
            copy.wait_recv()

    def arrive(g):
        landed(dealt(g))
        start(edges(g))
        ask(g).start()
        if g + EARLY < G:
            start(deal(g + EARLY))

    def make_bias(b, carry):
        lane = lax.broadcasted_iota(jnp.int32, (1, TOK), 1)
        key_first = (lane % COLS) < TC
        query_first = (lax.broadcasted_iota(jnp.int32, (TOK, TOK), 0) % COLS) < TC
        up = jnp.where(y * BANDS + b > 0, 1.0, 0.0).astype(F32)
        down = jnp.where(y * BANDS + b < 15, 1.0, 0.0).astype(F32)
        before = jnp.where(time < 7, 1.0, 0.0).astype(F32)
        for which, (table, base) in enumerate(((flags_in, 9), (flags_next, 0))):
            mask = table[b]
            for slot in range(3):
                lines = []
                for cq in range(2):
                    pair = []
                    for ck in range(2):
                        dw = ck - cq + 1
                        code = base + slot * 3 + dw
                        value = mask[cq:cq + 1, code:code + 1]
                        if which == 0 and slot == 1 and dw == 1:
                            value = jnp.ones_like(value)
                        if slot == 0:
                            value = value * up
                        if slot == 2:
                            value = value * down
                        if which == 1:
                            value = value * before
                        pair.append(value)
                    lines.append(jnp.where(key_first, pair[0], pair[1]))
                allowed = jnp.where(query_first, lines[0], lines[1])
                bias[b, which * TOK:(which + 1) * TOK, slot * TOK:(slot + 1) * TOK] = jnp.where(
                    allowed > 0.5, 0.0, MASKED
                )
        return carry

    contract = (((1,), (1,)), ((), ()))

    def window(g):
        landed(edges(g))
        ask(g).wait_recv()
        lane = lax.broadcasted_iota(jnp.int32, (TOK, 128), 1)
        table = jnp.zeros((TOK, 128), F32)
        for b in range(BANDS):
            q = jnp.concatenate([q_in[g, b], q_next[g, b]], axis=0)
            k = kv[g, 0, b:b + 3].reshape(3 * TOK, HD)
            v = kv[g, 1, b:b + 3].reshape(3 * TOK, HD)
            scores = lax.dot_general(q, k, contract, preferred_element_type=F32) + bias[b]
            top = jnp.max(scores, axis=1, keepdims=True)
            probs = jnp.exp2((scores - top) * SCALE).astype(BF16)
            total = jnp.dot(probs, jnp.concatenate([v, ones[0:3 * TOK]], axis=1), preferred_element_type=F32)
            weighted, norm = total[:, :HD], total[:, HD:]
            ours[g, b] = weighted[:TOK]
            our_sum[g, b] = norm[:TOK]
            our_top[g, b] = jnp.broadcast_to(top[:TOK], (TOK, HD))
            part[g, b] = (weighted[TOK:] / norm[TOK:]).astype(BF16)
            table = jnp.where(lane == b, top[TOK:], jnp.where(lane == b + 4, norm[TOK:], table))
        stat[g] = table.T[0:8]
        start(answer(g))

    def finish(g):
        landed(answer(g))
        table = jnp.concatenate([stat_in[g], jnp.zeros((120, 128), F32)], axis=0).T
        lines = slice(g * HD, (g + 1) * HD)
        sink_k = skv[:, :, 0, :, lines].reshape(512, HD)
        sink_v = jnp.concatenate([skv[:, :, 1, :, lines].reshape(512, HD), ones[...]], axis=1)
        for b in range(BANDS):
            scores = lax.dot_general(q_in[g, b], sink_k, contract, preferred_element_type=F32)
            top_a, top_b, norm_b = our_top[g, b], table[:, b:b + 1], table[:, b + 4:b + 5]
            top = jnp.maximum(jnp.maximum(top_a, top_b), jnp.max(scores, axis=1, keepdims=True))
            probs = jnp.exp2((scores - top[:, 0:1]) * SCALE).astype(BF16)
            total = jnp.dot(probs, sink_v, preferred_element_type=F32)
            weight_a = jnp.exp2((top_a - top) * SCALE)
            weight_b = jnp.exp2((top_b - top) * SCALE) * norm_b
            norm = weight_a * our_sum[g, b] + weight_b + total[:, HD:]
            value = weight_a * ours[g, b] + weight_b * back[g, b].astype(F32) + total[:, :HD]
            outs[g, b] = (value / norm).astype(BF16)
        start(out_copies(g))

    start(sink_x)
    start(flag_copies)
    for g in range(EARLY):
        start(deal(g))
    xin[x] = sel[:, :, own_lanes(x)]
    for i, d in enumerate((-1, 1, 2)):
        remote(xin.at[0], xin.at[(x + d + 4) % 4], sx_s.at[i], sx_r.at[i], partner).wait_recv()
    for i in range(2):
        zown[:, i * SINK:(i + 1) * SINK] = (xin[2 * i].astype(F32) + xin[2 * i + 1].astype(F32)).astype(BF16)
    start(sink_z)
    for b in range(BANDS):
        remote(flags, flags_in.at[b], fx_s.at[0], fx_r.at[b], partner).wait_recv()
    flag_next.start()
    arrive(0)
    landed(sink_z)
    skv[0, 0] = (zown[...].astype(F32) + zin[0].astype(F32) + zin[1].astype(F32) + zin[2].astype(F32)).astype(BF16)
    start(sink_y)
    sink_c[0].start()
    flag_next.wait_recv()
    lax.fori_loop(0, BANDS, make_bias, 0)
    arrive(1)
    window(0)
    arrive(2)
    window(1)
    for i in range(3):
        sink_y[i].wait_recv()
        sink_c[i + 1].start()
    arrive(3)
    window(2)
    landed(sink_c)
    finish(0)
    arrive(4)
    window(3)
    finish(1)
    window(4)
    finish(2)
    finish(3)
    finish(4)

    for g in range(G):
        for i in range(4):
            remote(outs.at[g, 0], out_ref.at[:, pl.ds(i * GE + g * HD, HD)], o_s.at[g, 0], o_r.at[g, i], partner).wait_recv()
    sent = [*sink_x, *sink_z, *sink_y, *sink_c, *flag_copies, flag_next]
    for g in range(G):
        sent += [*deal(g), *edges(g), ask(g), *answer(g), *out_copies(g)]
    for copy in sent:
        copy.wait_send()


def shards(queries, keys, values, tile_mask, sink_frame):
    any_spec, vmem, smem = (pl.BlockSpec(memory_space=space) for space in (pl.ANY, pltpu.VMEM, pltpu.SMEM))
    sems = pltpu.SemaphoreType.DMA
    bf = lambda *shape: pltpu.VMEM(shape, BF16)
    f32 = lambda *shape: pltpu.VMEM(shape, F32)
    pairs = [
        (4,), (), (G, 4), (G, 4), (G, 2), (G,), (G,), (G,), (3,), (3,), (3,), (4,), (G, 4),
    ]
    out = pl.pallas_call(
        attend,
        out_shape=jax.ShapeDtypeStruct((TOK, E), BF16),
        in_specs=[any_spec, any_spec, any_spec, any_spec, smem],
        out_specs=vmem,
        scratch_shapes=[
            pltpu.VMEM((2, 18), jnp.int32),
            bf(TOK, E), bf(2, TOK, E),
            f32(8, 128), f32(BANDS, 8, 128), f32(BANDS, 8, 128),
            f32(BANDS, 2 * TOK, 3 * TOK),
            bf(2, SINK, E), bf(4, 2, SINK, GE), bf(2, 2 * SINK, GE), bf(3, 2, 2 * SINK, GE),
            bf(4, 2, 2, 2 * SINK, GE), bf(512, HD),
            bf(G, BANDS, TOK, HD), bf(G, BANDS, TOK, HD), bf(G, 2, BANDS + 2, TOK, HD),
            bf(G, BANDS, TOK, HD), bf(G, BANDS, TOK, HD), f32(G, 8, 128), f32(G, 8, 128),
            f32(G, BANDS, TOK, HD), f32(G, BANDS, TOK, HD), f32(G, BANDS, TOK, HD), bf(G, BANDS, TOK, HD),
            sems((4,)),
            *[sems(shape) for shape in pairs for _ in range(2)],
        ],
        compiler_params=pltpu.CompilerParams(
            collective_id=0, has_side_effects=True, vmem_limit_bytes=60 * 2**20
        ),
        cost_estimate=pl.CostEstimate(flops=2 * 10**9, bytes_accessed=3 * 10**6, transcendentals=4 * 10**6),
    )(
        queries.reshape(TOK, E), keys.reshape(TOK, E), values.reshape(TOK, E),
        tile_mask.reshape(2, 18), sink_frame,
    )
    return out.reshape(queries.shape)


def solution(mesh):
    spec = P("tm", "height", None, None)
    return jax.shard_map(
        shards,
        mesh=mesh,
        in_specs=(spec, spec, spec, spec, P()),
        out_specs=spec,
        check_vma=False,
    )
```

time: 74 us -> 60.4 us (0.82)
  Pallas kernels: 68 us -> 57.6 us
  local copies, waits for them, and re-layouts: 4.77 us -> 1.97 us
    pallas_call x1, Pallas kernels: 68 us -> 57.6 us  [shards(): pl.pallas_call(attend, out_shape=jax.ShapeDtypeStruct((TOK, E), BF16), in...]
    unnamed x9 -> x1, local copies, waits for them, and re-layouts: 4.77 us -> 1.97 us
where the time goes in v2:
time: 60.4 us; the launch traced here: 60.2 us
  Pallas kernels  57.6 us (95%)
  local copies, waits for them, and re-layouts  1.97 us (3%)
  between operations  0.66 us (1%)
    pallas_call x1, Pallas kernels, shards(): pl.pallas_call(attend, out_shape=jax.ShapeDtypeStruct((TOK, E), BF16), in...  57.6 us
    unnamed x1, local copies, waits for them, and re-layouts  1.97 us

profile of v2, /device:TPU:1, one launch (start us, length us, event | category | flops | bytes accessed | tf_op | source)
XLA Modules:
  0.0 60.2 jit_solution(7312400427450201475)
XLA Ops:
  0.7 57.6 %shard_map.55 = bf16[128,2560]{1,0:T(8,128)(2,1)} custom-call(bf16[128,2560]{1,0:T(8,128)(2,1)} %bitcast.6, bf16[128,2560]{1,0:T(8,128)(2,1)} %bitcast.7, bf16[128,2560]{1,0:T(8,128)(2,1)} %bitcast.8, s32[2,18]{1,0:T(2,128)} %bitcast.9, s32[1]{0:T(128)S(6)} %copy.7.sink_ref), custom_call_target="tpu_custom_call" | custom-call | flops 2000000000 | bytes 3000000 | tf_op jit(solution)/shard_map/pallas_call | solution.py:315
  58.2 2.0 %copy.8 = bf16[4,2,16,2560]{3,2,1,0:T(8,128)(2,1)} copy(bf16[4,2,16,2560]{3,2,1,0:T(8,128)(2,1)} %bitcast.5) | data formatting | bytes 1310720

commit v3 on v2

v3 whole, which is shorter than its diff:
```python
import math

import jax
import jax.numpy as jnp
from jax import lax
from jax.experimental import pallas as pl
from jax.experimental.pallas import tpu as pltpu
from jax.sharding import PartitionSpec as P

H = 20
HD = 128
TF = 4
TC = 8
COLS = 16
E = H * HD
TOK = 128
SINK = 32
G = 5
GE = G * HD
BANDS = 4
EARLY = 2
MASKED = -1e30
SCALE = math.log2(math.e) / math.sqrt(HD)
MESH = pl.DeviceIdType.MESH
F32, BF16 = jnp.float32, jnp.bfloat16


def attend(q_hbm, k_hbm, v_hbm, mask_hbm, sink_ref, out_ref,
           mask_ref, ksrc, vsrc, flags, flags_in, flags_next, bias, sel, xin, skv, ones,
           q_in, q_next, kv, part, back, stat, stat_in, ours, our_top, our_sum, outs,
           local_sem, fx_s, fx_r, fz_s, fz_r, k_s, k_r, v_s, v_r, q_s, q_r, y_s, y_r, n_s, n_r, b_s, b_r, st_s, st_r,
           sx_s, sx_r, sy_s, sy_r, sc_s, sc_r, o_s, o_r):
    tm, h = lax.axis_index("tm"), lax.axis_index("height")
    lo, z, y, hi, c = tm // 4, tm % 4, h // 4, (h // 2) % 2, h % 2
    x = hi * 2 + lo
    time = z + 4 * c

    def at(x, y, z, c):
        x, y, z = (x + 4) % 4, (y + 4) % 4, (z + 4) % 4
        return ((x % 2) * 4 + z, y * 4 + (x // 2) * 2 + c)

    def at_time(t):
        t = (t + 8) % 8
        return at(x, y, t % 4, t // 4)

    partner = at(x, y, z, 1 - c)
    earlier, later = at_time(time - 1), at_time(time + 1)
    steps = (1, -1, 2)
    y_mates = [at(x, y + d, z, c) for d in steps]
    around = [(i, j) for i in (0, 1, -1, 2) for j in (0, 1, -1, 2) if (i, j) != (0, 0)]

    def remote(src, dst, send, recv, device):
        return pltpu.make_async_remote_copy(src, dst, send, recv, device_id=device, device_id_type=MESH)

    barrier = pltpu.get_barrier_semaphore()
    friends = [at(x + d, y, z, 1 - c) for d in steps]
    friends += [partner, earlier, later]
    friends += [at(x + dx, y, z + dz, c) for dx, dz in around]
    friends += [at(x, y + dy, z + dz, c) for dy, dz in around]
    for friend in friends:
        pl.semaphore_signal(barrier, inc=1, device_id=friend, device_id_type=MESH)
    local = [
        pltpu.make_async_copy(mask_hbm, mask_ref, local_sem.at[0]),
        pltpu.make_async_copy(k_hbm, ksrc, local_sem.at[1]),
        pltpu.make_async_copy(v_hbm, vsrc, local_sem.at[2]),
    ]
    for copy in local:
        copy.start()
    ones[...] = jnp.ones_like(ones)
    stat[...] = jnp.zeros_like(stat)
    flags[...] = jnp.zeros_like(flags)
    local[0].wait()
    flags[0:2, 0:18] = mask_ref[...].astype(F32)

    frame = (sink_ref[0] - tm * TF).astype(F32)
    for i, source in enumerate((ksrc, vsrc)):
        local[i + 1].wait()
        tokens = 0.0
        for f in range(TF):
            mine = jnp.where(frame == f, 1.0, 0.0).astype(F32)
            tokens = tokens + source[f * SINK:(f + 1) * SINK, :].astype(F32) * mine
        sel[i] = tokens.astype(BF16)
    pl.semaphore_wait(barrier, len(friends))

    def own_lanes(xx):
        return pl.ds(pl.multiple_of(((xx + 4) % 4) * GE, HD), GE)

    band = hi * 2 + c

    class Either:
        def __init__(self, src, dst, send, recv, device, here):
            self.far = lambda: remote(src, dst, send, recv, device)
            self.near = lambda: pltpu.make_async_copy(src, dst, recv)
            self.here = here

        def start(self):
            pl.when(self.here)(lambda: self.near().start())
            pl.when(jnp.logical_not(self.here))(lambda: self.far().start())

        def wait_send(self):
            pl.when(jnp.logical_not(self.here))(lambda: self.far().wait_send())

        def wait_recv(self):
            self.far().wait_recv()

    def fan(make):
        copies = [make(i, x + d, at(x + d, y, z, lo), remote) for i, d in enumerate(steps)]
        here = c == lo

        def either(*args):
            return Either(*args, here)

        return copies + [make(3, x, partner, either)]

    def deal(g):
        def lanes(xx):
            return pl.ds(pl.multiple_of(((xx + 4) % 4) * GE + g * HD, HD), HD)

        def of_k(i, xx, device, how):
            return how(k_hbm.at[:, lanes(xx)], kv.at[g, 0, band + 1], k_s.at[g, i], k_r.at[g, band], device)

        def of_v(i, xx, device, how):
            return how(v_hbm.at[:, lanes(xx)], kv.at[g, 1, band + 1], v_s.at[g, i], v_r.at[g, band], device)

        def of_q(i, xx, device, how):
            return how(q_hbm.at[:, lanes(xx)], q_in.at[g, band], q_s.at[g, i], q_r.at[g, band], device)

        return fan(of_k) + fan(of_v) + fan(of_q)

    def dealt(g):
        sample = k_hbm.at[:, pl.ds(0, HD)]
        copies = []
        for b in range(BANDS):
            copies += [
                remote(sample, kv.at[g, 0, b + 1], k_s.at[g, 0], k_r.at[g, b], partner),
                remote(sample, kv.at[g, 1, b + 1], v_s.at[g, 0], v_r.at[g, b], partner),
                remote(sample, q_in.at[g, b], q_s.at[g, 0], q_r.at[g, b], partner),
            ]
        return copies

    def edges(g):
        return [
            remote(kv.at[g, :, 4], kv.at[g, :, 0], y_s.at[g, 0], y_r.at[g, 0], y_mates[0]),
            remote(kv.at[g, :, 1], kv.at[g, :, 5], y_s.at[g, 1], y_r.at[g, 1], y_mates[1]),
        ]

    def ask(g):
        return remote(q_in.at[g], q_next.at[g], n_s.at[g], n_r.at[g], earlier)

    def answer(g, half):
        bands = pl.ds(2 * half, 2)
        return [
            remote(part.at[g, bands], back.at[g, bands], b_s.at[g, half], b_r.at[g, half], later),
            remote(stat.at[g, half], stat_in.at[g, half], st_s.at[g, half], st_r.at[g, half], later),
        ]

    def out_copies(g, half):
        copies = []
        for b in (2 * half, 2 * half + 1):
            xx, core = (b // 2) * 2 + c, b % 2
            copies.append(Either(
                outs.at[g, b], out_ref.at[:, pl.ds(pl.multiple_of(x * GE + g * HD, HD), HD)],
                o_s.at[g, b], o_r.at[g, x], at(xx, y, z, core), (xx == x) & (c == core),
            ))
        return copies

    flag_copies = fan(lambda i, xx, device, how: how(flags, flags_in.at[band], fx_s.at[i], fx_r.at[band], device))
    flag_next = remote(flags_in, flags_next, fz_s, fz_r, earlier)
    def piece_for(xx, zz):
        xx, zz = (xx + 4) % 4, (zz + 4) % 4
        rows = pl.ds(pl.multiple_of(zz % 2 * COLS, COLS), COLS)
        return sel.at[zz // 2, rows, pl.ds(pl.multiple_of(xx * GE, HD), GE)]

    def place_of(yy, zz):
        yy, zz = (yy + 4) % 4, (zz + 4) % 4
        return skv.at[yy, 0, zz // 2, zz % 2]

    sink_x = [
        remote(piece_for(x + dx, z + dz), xin.at[x, z], sx_s.at[n], sx_r.at[n], at(x + dx, y, z + dz, c))
        for n, (dx, dz) in enumerate(around)
    ]
    sink_y = [
        remote(place_of(y, z), place_of(y, z), sy_s.at[n], sy_r.at[n], at(x, y + dy, z + dz, c))
        for n, (dy, dz) in enumerate(around)
    ]

    def across(i):
        yy = (y - (0, 1, -1, 2)[i] + 4) % 4
        return remote(skv.at[yy, 0], skv.at[yy, 1], sc_s.at[i], sc_r.at[i], partner)

    def pass_on():
        for i, dy in enumerate((0, 1, -1, 2)):
            for n, offset in enumerate(around):
                if offset[0] == dy:
                    sink_y[n].wait_recv()
            across(i).start()

    def start(copies):
        for copy in copies:
            copy.start()

    def landed(copies):
        for copy in copies:
            copy.wait_recv()

    def arrive(g):
        landed(dealt(g))
        start(edges(g))
        ask(g).start()
        if g + EARLY < G:
            start(deal(g + EARLY))

    def make_bias(b, carry):
        lane = lax.broadcasted_iota(jnp.int32, (1, TOK), 1)
        key_first = (lane % COLS) < TC
        query_first = (lax.broadcasted_iota(jnp.int32, (TOK, TOK), 0) % COLS) < TC
        up = jnp.where(y * BANDS + b > 0, 1.0, 0.0).astype(F32)
        down = jnp.where(y * BANDS + b < 15, 1.0, 0.0).astype(F32)
        before = jnp.where(time < 7, 1.0, 0.0).astype(F32)
        for which, (table, base) in enumerate(((flags_in, 9), (flags_next, 0))):
            mask = table[b]
            for slot in range(3):
                lines = []
                for cq in range(2):
                    pair = []
                    for ck in range(2):
                        dw = ck - cq + 1
                        code = base + slot * 3 + dw
                        value = mask[cq:cq + 1, code:code + 1]
                        if which == 0 and slot == 1 and dw == 1:
                            value = jnp.ones_like(value)
                        if slot == 0:
                            value = value * up
                        if slot == 2:
                            value = value * down
                        if which == 1:
                            value = value * before
                        pair.append(value)
                    lines.append(jnp.where(key_first, pair[0], pair[1]))
                allowed = jnp.where(query_first, lines[0], lines[1])
                bias[b, which * TOK:(which + 1) * TOK, slot * TOK:(slot + 1) * TOK] = jnp.where(
                    allowed > 0.5, 0.0, MASKED
                )
        return carry

    contract = (((1,), (1,)), ((), ()))

    def window(g):
        landed(edges(g))
        ask(g).wait_recv()
        lane = lax.broadcasted_iota(jnp.int32, (TOK, 128), 1)
        for half in range(2):
            table = jnp.zeros((TOK, 128), F32)
            for b in (2 * half, 2 * half + 1):
                q = jnp.concatenate([q_in[g, b], q_next[g, b]], axis=0)
                k = kv[g, 0, b:b + 3].reshape(3 * TOK, HD)
                v = kv[g, 1, b:b + 3].reshape(3 * TOK, HD)
                scores = lax.dot_general(q, k, contract, preferred_element_type=F32) + bias[b]
                top = jnp.max(scores, axis=1, keepdims=True)
                probs = jnp.exp2((scores - top) * SCALE).astype(BF16)
                total = jnp.dot(probs, jnp.concatenate([v, ones[0:3 * TOK]], axis=1), preferred_element_type=F32)
                weighted, norm = total[:, :HD], total[:, HD:]
                ours[g, b] = weighted[:TOK]
                our_sum[g, b] = norm[:TOK]
                our_top[g, b] = jnp.broadcast_to(top[:TOK], (TOK, HD))
                part[g, b] = (weighted[TOK:] / norm[TOK:]).astype(BF16)
                table = jnp.where(lane == b % 2, top[TOK:], jnp.where(lane == b % 2 + 4, norm[TOK:], table))
            stat[g, half] = table.T[0:8]
            start(answer(g, half))

    def finish(g):
        lines = slice(g * HD, (g + 1) * HD)
        sink_k = skv[:, :, 0, :, :, :, lines].reshape(512, HD)
        sink_v = jnp.concatenate([skv[:, :, 1, :, :, :, lines].reshape(512, HD), ones[...]], axis=1)
        for half in range(2):
            landed(answer(g, half))
            table = jnp.concatenate([stat_in[g, half], jnp.zeros((120, 128), F32)], axis=0).T
            for b in (2 * half, 2 * half + 1):
                scores = lax.dot_general(q_in[g, b], sink_k, contract, preferred_element_type=F32)
                top_a, top_b, norm_b = our_top[g, b], table[:, b % 2:b % 2 + 1], table[:, b % 2 + 4:b % 2 + 5]
                top = jnp.maximum(jnp.maximum(top_a, top_b), jnp.max(scores, axis=1, keepdims=True))
                probs = jnp.exp2((scores - top[:, 0:1]) * SCALE).astype(BF16)
                total = jnp.dot(probs, sink_v, preferred_element_type=F32)
                weight_a = jnp.exp2((top_a - top) * SCALE)
                weight_b = jnp.exp2((top_b - top) * SCALE) * norm_b
                norm = weight_a * our_sum[g, b] + weight_b + total[:, HD:]
                value = weight_a * ours[g, b] + weight_b * back[g, b].astype(F32) + total[:, :HD]
                outs[g, b] = (value / norm).astype(BF16)
            start(out_copies(g, half))

    start(flag_copies)
    start(sink_x)
    start(deal(0))
    for g in range(1, EARLY):
        start(deal(g))
    xin[x, z] = piece_for(x, z)[...]
    landed(sink_x)
    for i in range(2):
        total = sum(xin[2 * i + j, k].astype(F32) for j in range(2) for k in range(4))
        skv[y, 0, z // 2, z % 2, i] = total.astype(BF16)
    start(sink_y)
    for b in range(BANDS):
        remote(flags, flags_in.at[b], fx_s.at[0], fx_r.at[b], partner).wait_recv()
    flag_next.start()
    arrive(0)
    flag_next.wait_recv()
    lax.fori_loop(0, BANDS, make_bias, 0)
    arrive(1)
    window(0)
    arrive(2)
    window(1)
    pass_on()
    arrive(3)
    window(2)
    landed([across(i) for i in range(4)])
    finish(0)
    arrive(4)
    window(3)
    finish(1)
    window(4)
    finish(2)
    finish(3)
    finish(4)

    for g in range(G):
        for i in range(4):
            remote(outs.at[g, 0], out_ref.at[:, pl.ds(i * GE + g * HD, HD)], o_s.at[g, 0], o_r.at[g, i], partner).wait_recv()
    sent = [*sink_x, *sink_y, *[across(i) for i in range(4)], *flag_copies, flag_next]
    for g in range(G):
        sent += [*deal(g), *edges(g), ask(g), *answer(g, 0), *answer(g, 1), *out_copies(g, 0), *out_copies(g, 1)]
    for copy in sent:
        copy.wait_send()


def shards(queries, keys, values, tile_mask, sink_frame):
    hbm, vmem, smem = (pl.BlockSpec(memory_space=space) for space in (pltpu.HBM, pltpu.VMEM, pltpu.SMEM))
    sems = pltpu.SemaphoreType.DMA
    bf = lambda *shape: pltpu.VMEM(shape, BF16)
    f32 = lambda *shape: pltpu.VMEM(shape, F32)
    pairs = [
        (4,), (), (G, 4), (G, 4), (G, 4), (G, 2), (G,), (G, 2), (G, 2), (15,), (15,), (4,), (G, 4),
    ]
    out = pl.pallas_call(
        attend,
        out_shape=jax.ShapeDtypeStruct((TOK, E), BF16),
        in_specs=[hbm, hbm, hbm, hbm, smem],
        out_specs=vmem,
        scratch_shapes=[
            pltpu.VMEM((2, 18), jnp.int32),
            bf(TOK, E), bf(TOK, E),
            f32(8, 128), f32(BANDS, 8, 128), f32(BANDS, 8, 128),
            f32(BANDS, 2 * TOK, 3 * TOK),
            bf(2, SINK, E), bf(4, 4, COLS, GE), bf(4, 2, 2, 2, 2, COLS, GE), bf(512, HD),
            bf(G, BANDS, TOK, HD), bf(G, BANDS, TOK, HD), bf(G, 2, BANDS + 2, TOK, HD),
            bf(G, BANDS, TOK, HD), bf(G, BANDS, TOK, HD), f32(G, 2, 8, 128), f32(G, 2, 8, 128),
            f32(G, BANDS, TOK, HD), f32(G, BANDS, TOK, HD), f32(G, BANDS, TOK, HD), bf(G, BANDS, TOK, HD),
            sems((4,)),
            *[sems(shape) for shape in pairs for _ in range(2)],
        ],
        compiler_params=pltpu.CompilerParams(
            collective_id=0, has_side_effects=True, vmem_limit_bytes=32 * 2**20
        ),
        cost_estimate=pl.CostEstimate(flops=2 * 10**9, bytes_accessed=3 * 10**6, transcendentals=4 * 10**6),
    )(
        *(pltpu.with_memory_space_constraint(a, pltpu.HBM) for a in (
            queries.reshape(TOK, E), keys.reshape(TOK, E), values.reshape(TOK, E), tile_mask.reshape(2, 18))),
        sink_frame,
    )
    return out.reshape(queries.shape)


def solution(mesh):
    spec = P("tm", "height", None, None)
    return jax.shard_map(
        shards,
        mesh=mesh,
        in_specs=(spec, spec, spec, spec, P()),
        out_specs=spec,
        check_vma=False,
    )
```

time: 60.4 us -> 55.2 us (0.914)
  Pallas kernels: 57.6 us -> 53.6 us
  local copies, waits for them, and re-layouts: 1.97 us -> 0.84 us
    pallas_call x1, Pallas kernels: 57.6 us -> 53.6 us  [shards(): pl.pallas_call(attend, out_shape=jax.ShapeDtypeStruct((TOK, E), BF16), in...]
    unnamed x1, local copies, waits for them, and re-layouts: 1.97 us -> 0.84 us
where the time goes in v3:
time: 55.2 us; the launch traced here: 55.1 us
  Pallas kernels  53.6 us (97%)
  local copies, waits for them, and re-layouts  0.84 us (2%)
  between operations  0.66 us (1%)
    pallas_call x1, Pallas kernels, shards(): pl.pallas_call(attend, out_shape=jax.ShapeDtypeStruct((TOK, E), BF16), in...  53.6 us

profile of v3, /device:TPU:1, one launch (start us, length us, event | category | flops | bytes accessed | tf_op | source)
XLA Modules:
  0.0 55.1 jit_solution(15829322679584992452)
XLA Ops:
  0.7 53.6 %shard_map.55 = bf16[128,2560]{1,0:T(8,128)(2,1)S(1)} custom-call(bf16[128,2560]{1,0:T(8,128)(2,1)} %bitcast.6, bf16[128,2560]{1,0:T(8,128)(2,1)} %bitcast.7, bf16[128,2560]{1,0:T(8,128)(2,1)} %bitcast.8, s32[2,18]{1,0:T(2,128)} %bitcast.9, s32[1]{0:T(128)S(6)} %copy.7.sink_ref), custom_call_target="tpu_custom_call" | custom-call | flops 2000000000 | bytes 3000000 | tf_op jit(solution)/shard_map/pallas_call | solution.py:343
  54.2 0.8 %copy.8 = bf16[4,2,16,2560]{3,2,1,0:T(8,128)(2,1)} copy(bf16[4,2,16,2560]{3,2,1,0:T(8,128)(2,1)S(1)} %bitcast.5) | data formatting | bytes 1310720

commit v4 on v3

--- a/solution.py
+++ b/solution.py
@@ -56,7 +56,7 @@
     friends = [at(x + d, y, z, 1 - c) for d in steps]
     friends += [partner, earlier, later]
     friends += [at(x + dx, y, z + dz, c) for dx, dz in around]
-    friends += [at(x, y + dy, z + dz, c) for dy, dz in around]
+    friends += [at(x, y + dy, z + dz, c) for dy, dz in around if dy != 0]
     for friend in friends:
         pl.semaphore_signal(barrier, inc=1, device_id=friend, device_id_type=MESH)
     local = [
@@ -250,23 +250,31 @@
         ask(g).wait_recv()
         lane = lax.broadcasted_iota(jnp.int32, (TOK, 128), 1)
         for half in range(2):
+            bands = (2 * half, 2 * half + 1)
+            scores = [
+                lax.dot_general(
+                    jnp.concatenate([q_in[g, b], q_next[g, b]], axis=0), kv[g, 0, b:b + 3].reshape(3 * TOK, HD),
+                    contract, preferred_element_type=F32,
+                ) + bias[b]
+                for b in bands
+            ]
+            tops = [jnp.max(score, axis=1, keepdims=True) for score in scores]
+            probs = [jnp.exp2((score - top) * SCALE).astype(BF16) for score, top in zip(scores, tops)]
+            totals = [
+                jnp.dot(prob, jnp.concatenate([kv[g, 1, b:b + 3].reshape(3 * TOK, HD), ones[0:3 * TOK]], axis=1),
+                        preferred_element_type=F32)
+                for prob, b in zip(probs, bands)
+            ]
             table = jnp.zeros((TOK, 128), F32)
-            for b in (2 * half, 2 * half + 1):
-                q = jnp.concatenate([q_in[g, b], q_next[g, b]], axis=0)
-                k = kv[g, 0, b:b + 3].reshape(3 * TOK, HD)
-                v = kv[g, 1, b:b + 3].reshape(3 * TOK, HD)
-                scores = lax.dot_general(q, k, contract, preferred_element_type=F32) + bias[b]
-                top = jnp.max(scores, axis=1, keepdims=True)
-                probs = jnp.exp2((scores - top) * SCALE).astype(BF16)
-                total = jnp.dot(probs, jnp.concatenate([v, ones[0:3 * TOK]], axis=1), preferred_element_type=F32)
-                weighted, norm = total[:, :HD], total[:, HD:]
-                ours[g, b] = weighted[:TOK]
-                our_sum[g, b] = norm[:TOK]
-                our_top[g, b] = jnp.broadcast_to(top[:TOK], (TOK, HD))
-                part[g, b] = (weighted[TOK:] / norm[TOK:]).astype(BF16)
-                table = jnp.where(lane == b % 2, top[TOK:], jnp.where(lane == b % 2 + 4, norm[TOK:], table))
+            for i, (b, top, total) in enumerate(zip(bands, tops, totals)):
+                part[g, b] = (total[TOK:, :HD] / total[TOK:, HD:]).astype(BF16)
+                table = jnp.where(lane == i, top[TOK:], jnp.where(lane == i + 4, total[TOK:, HD:], table))
             stat[g, half] = table.T[0:8]
             start(answer(g, half))
+            for b, top, total in zip(bands, tops, totals):
+                ours[g, b] = total[:TOK, :HD]
+                our_sum[g, b] = total[:TOK, HD:]
+                our_top[g, b] = jnp.broadcast_to(top[:TOK], (TOK, HD))
 
     def finish(g):
         lines = slice(g * HD, (g + 1) * HD)
@@ -275,17 +283,25 @@
         for half in range(2):
             landed(answer(g, half))
             table = jnp.concatenate([stat_in[g, half], jnp.zeros((120, 128), F32)], axis=0).T
-            for b in (2 * half, 2 * half + 1):
-                scores = lax.dot_general(q_in[g, b], sink_k, contract, preferred_element_type=F32)
-                top_a, top_b, norm_b = our_top[g, b], table[:, b % 2:b % 2 + 1], table[:, b % 2 + 4:b % 2 + 5]
-                top = jnp.maximum(jnp.maximum(top_a, top_b), jnp.max(scores, axis=1, keepdims=True))
-                probs = jnp.exp2((scores - top[:, 0:1]) * SCALE).astype(BF16)
-                total = jnp.dot(probs, sink_v, preferred_element_type=F32)
-                weight_a = jnp.exp2((top_a - top) * SCALE)
-                weight_b = jnp.exp2((top_b - top) * SCALE) * norm_b
-                norm = weight_a * our_sum[g, b] + weight_b + total[:, HD:]
-                value = weight_a * ours[g, b] + weight_b * back[g, b].astype(F32) + total[:, :HD]
-                outs[g, b] = (value / norm).astype(BF16)
+            bands = pl.ds(2 * half, 2)
+            scores = lax.dot_general(
+                q_in[g, bands].reshape(2 * TOK, HD), sink_k, contract, preferred_element_type=F32
+            )
+            top_a, top_b, norm_b = (
+                our_top[g, bands].reshape(2 * TOK, HD),
+                *(jnp.concatenate([table[:, i:i + 1], table[:, i + 1:i + 2]], axis=0) for i in (0, 4)),
+            )
+            top = jnp.maximum(jnp.maximum(top_a, top_b), jnp.max(scores, axis=1, keepdims=True))
+            probs = jnp.exp2((scores - top[:, 0:1]) * SCALE).astype(BF16)
+            total = jnp.dot(probs, sink_v, preferred_element_type=F32)
+            weight_a = jnp.exp2((top_a - top) * SCALE)
+            weight_b = jnp.exp2((top_b - top) * SCALE) * norm_b
+            norm = weight_a * our_sum[g, bands].reshape(2 * TOK, HD) + weight_b + total[:, HD:]
+            value = (
+                weight_a * ours[g, bands].reshape(2 * TOK, HD)
+                + weight_b * back[g, bands].reshape(2 * TOK, HD).astype(F32) + total[:, :HD]
+            )
+            outs[g, bands] = (value / norm).astype(BF16).reshape(2, TOK, HD)
             start(out_copies(g, half))
 
     start(flag_copies)
@@ -312,24 +328,30 @@
     pass_on()
     arrive(3)
     window(2)
+    arrive(4)
     landed([across(i) for i in range(4)])
     finish(0)
-    arrive(4)
     window(3)
     finish(1)
     window(4)
     finish(2)
+    sent = [*sink_x, *sink_y, *[across(i) for i in range(4)], *flag_copies, flag_next]
+    for g in range(G):
+        sent += [*deal(g), *edges(g), ask(g)]
+    for g in range(2):
+        sent += [*answer(g, 0), *answer(g, 1), *out_copies(g, 0), *out_copies(g, 1)]
+    for copy in sent:
+        copy.wait_send()
     finish(3)
     finish(4)
 
     for g in range(G):
         for i in range(4):
             remote(outs.at[g, 0], out_ref.at[:, pl.ds(i * GE + g * HD, HD)], o_s.at[g, 0], o_r.at[g, i], partner).wait_recv()
-    sent = [*sink_x, *sink_y, *[across(i) for i in range(4)], *flag_copies, flag_next]
-    for g in range(G):
-        sent += [*deal(g), *edges(g), ask(g), *answer(g, 0), *answer(g, 1), *out_copies(g, 0), *out_copies(g, 1)]
-    for copy in sent:
-        copy.wait_send()
+    for g in range(2, G):
+        sent = [*answer(g, 0), *answer(g, 1), *out_copies(g, 0), *out_copies(g, 1)]
+        for copy in sent:
+            copy.wait_send()
 
 
 def shards(queries, keys, values, tile_mask, sink_frame):

time: 55.2 us -> 54.8 us (level)
  no operation moved by 1% of the time
where the time goes in v4:
time: 54.8 us; the launch traced here: 54.6 us
  Pallas kernels  53.1 us (97%)
  local copies, waits for them, and re-layouts  0.84 us (2%)
  between operations  0.66 us (1%)
    pallas_call x1, Pallas kernels, shards(): pl.pallas_call(attend, out_shape=jax.ShapeDtypeStruct((TOK, E), BF16), in...  53.1 us

profile of v4, /device:TPU:1, one launch (start us, length us, event | category | flops | bytes accessed | tf_op | source)
XLA Modules:
  0.0 54.6 jit_solution(2761181857374882849)
XLA Ops:
  0.7 53.1 %shard_map.55 = bf16[128,2560]{1,0:T(8,128)(2,1)S(1)} custom-call(bf16[128,2560]{1,0:T(8,128)(2,1)} %bitcast.6, bf16[128,2560]{1,0:T(8,128)(2,1)} %bitcast.7, bf16[128,2560]{1,0:T(8,128)(2,1)} %bitcast.8, s32[2,18]{1,0:T(2,128)} %bitcast.9, s32[1]{0:T(128)S(6)} %copy.7.sink_ref), custom_call_target="tpu_custom_call" | custom-call | flops 2000000000 | bytes 3000000 | tf_op jit(solution)/shard_map/pallas_call | solution.py:365
  53.8 0.8 %copy.8 = bf16[4,2,16,2560]{3,2,1,0:T(8,128)(2,1)} copy(bf16[4,2,16,2560]{3,2,1,0:T(8,128)(2,1)S(1)} %bitcast.5) | data formatting | bytes 1310720

commit v5 on v4

--- a/solution.py
+++ b/solution.py
@@ -104,7 +104,7 @@
             self.far().wait_recv()
 
     def fan(make):
-        copies = [make(i, x + d, at(x + d, y, z, lo), remote) for i, d in enumerate(steps)]
+        copies = [make(i, x + d, at(x + d, y, z, lo), remote) for i, d in ((2, 2), (0, 1), (1, -1))]
         here = c == lo
 
         def either(*args):

time: 54.8 us -> 54.4 us (level)
  no operation moved by 1% of the time
where the time goes in v5:
time: 54.4 us; the launch traced here: 54.2 us
  Pallas kernels  52.7 us (97%)
  local copies, waits for them, and re-layouts  0.84 us (2%)
  between operations  0.66 us (1%)
    pallas_call x1, Pallas kernels, shards(): pl.pallas_call(attend, out_shape=jax.ShapeDtypeStruct((TOK, E), BF16), in...  52.7 us

profile of v5, /device:TPU:1, one launch (start us, length us, event | category | flops | bytes accessed | tf_op | source)
XLA Modules:
  0.0 54.2 jit_solution(13186288460903805859)
XLA Ops:
  0.7 52.7 %shard_map.55 = bf16[128,2560]{1,0:T(8,128)(2,1)S(1)} custom-call(bf16[128,2560]{1,0:T(8,128)(2,1)} %bitcast.6, bf16[128,2560]{1,0:T(8,128)(2,1)} %bitcast.7, bf16[128,2560]{1,0:T(8,128)(2,1)} %bitcast.8, s32[2,18]{1,0:T(2,128)} %bitcast.9, s32[1]{0:T(128)S(6)} %copy.7.sink_ref), custom_call_target="tpu_custom_call" | custom-call | flops 2000000000 | bytes 3000000 | tf_op jit(solution)/shard_map/pallas_call | solution.py:365
  53.4 0.8 %copy.8 = bf16[4,2,16,2560]{3,2,1,0:T(8,128)(2,1)} copy(bf16[4,2,16,2560]{3,2,1,0:T(8,128)(2,1)S(1)} %bitcast.5) | data formatting | bytes 1310720
